TPU v7x, 128 devices: a whole 4x4x4 slice. The times are simulated.
128 devices in a mesh: section: 4 (over x), zone: 32 (over z, y, core).
Axes of the slice: x: 4, y: 4, z: 4, core: 2. Of those that a mesh axis runs over, the one named last changes fastest.
Arguments:
- tiles: bfloat16 [4, 4096, 128, 128], P('section', 'zone'), may hold values from -0.5 to 0.5
- tile_row: int32 [4, 4096], P('section', 'zone'), may hold values from 0 to 19
- tile_col: int32 [4, 4096], P('section', 'zone'), may hold values from 0 to 63, as said below
- tile_live: int32 [4, 4096], P('section', 'zone'), may hold values from 0 to 1, as said below
- block_place: int32 [64], replicated, may hold values from 0 to 63, as said below
- demand: int32 [4, 81920, 128], P('section', 'zone'), may hold values from 0 to 15
- flow_cost: float32 [4, 8192], P('section', 'zone'), may hold values from -6 to 6
- stock_cost: float32 [4, 81920], P('section', 'zone'), may hold values from 0.1 to 1
- flows: float32 [4, 8192, 128], P('section', 'zone'), may hold values from 0 to 1
- stock: float32 [4, 81920, 128], P('section', 'zone'), may hold values from 0 to 2
- duals: float32 [4, 81920, 128], P('section', 'zone'), may hold values from -6 to 6
Outputs:
- flows_out: float32 [4, 8192, 128], P('section', 'zone')
- stock_out: float32 [4, 81920, 128], P('section', 'zone')
- duals_out: float32 [4, 81920, 128], P('section', 'zone')
Inputs may be any that keep to these rules, and one draw needn't show every extreme that they name: `tile_col`: flow block ids. For each phase and zone band, at most 4 live slots name flow blocks whose position // 2 is one given band; in each phase one band receives exactly 4 such slots from every zone band. `tile_live`: live flags of the slots, with the counts described for tile_col. `block_place`: A permutation of the flow blocks.
All inputs are finite; a program needn't handle non-finite values.
Results may differ from a plain program's by a relative error of at most 0.019.
Values may be sent and summed in bfloat16 or wider, within the bound.
A program may use at most 128 MiB of HBM per device.

v0:
```python
import jax
import jax.numpy as jnp
from jax import lax
from jax.sharding import PartitionSpec as P

ITERS = 2
STEP_PRIMAL = 0.25
STEP_DUAL = 0.25


def from_behind(value, axis, by):
    size = lax.axis_size(axis)
    return lax.ppermute(value, axis, [(i, (i + by) % size) for i in range(size)])


def per_device(
    tiles,
    tile_row,
    tile_col,
    tile_live,
    block_place,
    demand,
    flow_cost,
    stock_cost,
    flows,
    stock,
    duals,
):
    phase_count, slot_count, tile_size, unused_size = tiles.shape
    scenarios = flows.shape[2]
    zone_count = lax.axis_size("zone")
    blocks_total = block_place.shape[0]
    block_local = blocks_total // zone_count
    band_tiles = duals.shape[1] // tile_size
    width_flat = tile_size * scenarios
    alive = tile_live == 1
    position = block_place[tile_col]
    demand_rhs = demand.astype(jnp.float32) * 0.25
    phase_ids = jnp.arange(phase_count, dtype=jnp.int32)[:, None]
    block_ids = jnp.where(alive, position, -1)
    row_live = jnp.where(alive, tile_row, band_tiles)
    for iteration in range(ITERS):
        dual_half = duals.astype(jnp.bfloat16).reshape(
            phase_count, band_tiles, tile_size, scenarios
        )
        dual_picked = jnp.take_along_axis(dual_half, tile_row[:, :, None, None], axis=1)
        partial_value = jnp.einsum(
            "snij,snic->snjc", tiles, dual_picked, preferred_element_type=jnp.float32
        )
        partial_value = partial_value.astype(jnp.bfloat16).reshape(
            phase_count, slot_count, width_flat
        )
        shifted = jnp.where(block_ids >= 0, block_ids, -1)
        shifted = jnp.where(shifted < lax.axis_size("zone") * block_local, shifted, -1)

        def one_phase(values, segment_ids):
            return jax.ops.segment_sum(
                values.astype(jnp.float32),
                segment_ids,
                num_segments=lax.axis_size("zone") * block_local,
            )

        summed_blocks = jax.vmap(one_phase)(partial_value, shifted)
        summed = lax.psum_scatter(
            jnp.transpose(summed_blocks, (1, 0, 2)), "zone", scatter_dimension=0, tiled=True
        )
        pulled = jnp.transpose(summed, (1, 0, 2))
        pulled = pulled.reshape(phase_count, block_local * tile_size, scenarios)
        dual_edge = from_behind(duals, "section", -1)
        dual_after = jnp.concatenate([duals[1:], dual_edge], axis=0)
        new_flows = jnp.maximum(flows - STEP_PRIMAL * (flow_cost[:, :, None] - pulled), 0.0)
        new_stock = jnp.maximum(
            stock - STEP_PRIMAL * (stock_cost[:, :, None] - dual_after + duals), 0.0
        )
        flows_bar = (2.0 * new_flows - flows).astype(jnp.bfloat16)
        stock_bar = 2.0 * new_stock - stock
        gathered = lax.all_gather(flows_bar, "zone", axis=1, tiled=True).reshape(
            phase_count, blocks_total, tile_size, scenarios
        )
        flow_picked = jnp.take_along_axis(gathered, position[:, :, None, None], axis=1)
        products = jnp.einsum(
            "snij,snjc->snic", tiles, flow_picked, preferred_element_type=jnp.float32
        )
        pushed = (
            jnp.zeros((phase_count, band_tiles, tile_size, scenarios), jnp.float32)
            .at[phase_ids, row_live]
            .add(products, mode="drop")
        )
        pushed = pushed.reshape(phase_count, band_tiles * tile_size, scenarios)
        stock_edge = from_behind(stock_bar, "section", 1)
        stock_before = jnp.concatenate([stock_edge, stock_bar[:-1]], axis=0)
        duals = duals + STEP_DUAL * (demand_rhs - (pushed + stock_before - stock_bar))
        flows = new_flows
        stock = new_stock
    return (flows, stock, duals)


def solution(mesh):
    in_specs = (
        P("section", "zone", None, None),
        P("section", "zone"),
        P("section", "zone"),
        P("section", "zone"),
        P(),
        P("section", "zone", None),
        P("section", "zone"),
        P("section", "zone"),
        P("section", "zone", None),
        P("section", "zone", None),
        P("section", "zone", None),
    )
    out_specs = (P("section", "zone", None), P("section", "zone", None), P("section", "zone", None))
    return jax.shard_map(
        per_device, mesh=mesh, in_specs=in_specs, out_specs=out_specs, check_vma=False
    )
```

profile of v0, /device:TPU:1, one launch (start us, length us, event | category | flops | bytes accessed | tf_op | source)
XLA Modules:
  0.0 547.1 jit_solution(18323352815189189794)
XLA Ops:
  7.2 0.0 copy-start
  7.2 0.0 all-reduce.6.cloned.1.call-start
  7.2 3.4 collective-permute-start
  10.6 0.7 fusion.52
  11.3 0.0 copy-done
  11.3 1.2 gather_fusion
  12.5 0.7 reduce
  13.2 0.7 fusion.54
  13.9 0.7 fusion.55
  14.6 0.7 and_bitcast_fusion.1
  15.3 23.1 %collective-permute-done = f32[1,2560,128]{2,1,0:T(8,128)} collective-permute-done((f32[1,2560,128]{2,1,0:T(8,128)}, f32[1,2560,128]{2,1,0:T(8,128)}, u32[]{:S(2)}, u32[]{:S(2)}) %collective-permute-start) | collective-permute-done | bytes 1310752 | tf_op jit(solution)/shard_map/ppermute | solution.py:13
  38.4 4.0 multiply_subtract_fusion.1
  42.3 3.1 gather_fusion.1
  45.4 8.4 %convert_bitcast_fusion.1 = f32[128,128,128]{1,2,0:T(8,128)} fusion(bf16[1,128,128,128]{3,2,1,0:T(8,128)(2,1)} %param.15, bf16[128,128,128]{2,1,0:T(8,128)(2,1)} %gather_fusion.1, pred[128]{0:T(512)(128)(4,1)S(1)} %and_bitcast_fusion.1), kind=kOutput, calls=%fused_computation.10 | convolution fusion | flops 543162368 | bytes 16777344 | tf_op jit(solution)/shard_map/snij,snic->snjc/dot_general | solution.py:47
  53.8 9.4 %copy.35 = f32[128,128,128]{0,2,1:T(8,128)} copy(f32[128,128,128]{1,2,0:T(8,128)} %convert_bitcast_fusion.1) | data formatting | bytes 16777216 | tf_op jit(solution)/shard_map/vmap()/convert_element_type | solution.py:58
  63.2 9.0 %copy.36 = f32[128,16384]{1,0:T(8,128)} copy(f32[128,16384]{0,1:T(8,128)} %bitcast.163) | data formatting | bytes 16777216 | tf_op jit(solution)/shard_map/vmap()/convert_element_type | solution.py:58
  72.2 0.0 copy-start.6
  72.2 15.1 %scatter_custom_fusion.2 = f32[64,16384]{1,0:T(8,128)} fusion(s32[128]{0:T(128)S(1)} %fusion.51, f32[128,16384]{1,0:T(8,128)} %copy.36, f32[]{:T(128)} %constant.3.clone.1), kind=kCustom, calls=%fused_computation.39 | custom fusion | flops 2097152 | bytes 4194816 | tf_op jit(solution)/shard_map/vmap()/scatter-add | solution.py:57
  87.3 0.0 all-reduce.6.cloned.1.call-update
  87.3 0.0 all-gather.3.cloned.1.call-start
  87.4 0.6 dynamic-slice
  88.6 114.6 %all-reduce.6.cloned.1.call-done = f32[64,1,16384]{2,0,1:T(8,128)} async-done(((f32[64,1,16384]{2,0,1:T(8,128)}), f32[64,1,16384]{2,0,1:T(8,128)}) %all-reduce.6.cloned.1.call-update) | async-done | bytes 4194320
  203.2 1.1 constant_dynamic-slice_fusion.1
  204.3 0.1 reshape_transpose.6
  204.4 0.7 subtract_convert_fusion.1
  205.2 0.0 all-gather.3.cloned.1.call-update
  205.2 0.0 all-reduce.8.cloned.1.call-start
  205.2 0.0 copy-done.3
  205.2 1.8 collective-permute-start.1
  207.1 0.0 copy-start.10
  207.1 42.9 %all-gather.3.cloned.1.call-done = bf16[1,8192,128]{2,1,0:T(8,128)(2,1)} async-done(((bf16[1,256,128]{2,1,0:T(8,128)(2,1)}), bf16[1,8192,128]{2,1,0:T(8,128)(2,1)}) %all-gather.3.cloned.1.call-update) | async-done | bytes 2097168 | tf_op jit(solution)/shard_map/all_gather | solution.py:77
  250.0 4.6 gather_fusion.2
  254.7 9.9 %fusion.20 = f32[128,128,128]{1,2,0:T(8,128)} fusion(bf16[1,128,128,128]{3,2,1,0:T(8,128)(2,1)} %param.15, bf16[128,128,128]{2,1,0:T(8,128)(2,1)} %gather_fusion.2, pred[128]{0:T(512)(128)(4,1)S(1)} %and_bitcast_fusion), kind=kOutput, calls=%fused_computation.31 | convolution fusion | flops 538968064 | bytes 16777344 | tf_op jit(solution)/shard_map/snij,snjc->snic/dot_general | solution.py:81
  264.6 9.0 %copy.38 = f32[128,128,128]{2,1,0:T(8,128)} copy(f32[128,128,128]{1,2,0:T(8,128)} %fusion.20) | data formatting | bytes 16777216 | tf_op jit(solution)/shard_map/snij,snjc->snic/dot_general | solution.py:81
  273.6 0.1 broadcast.166.clone
  273.7 17.0 %scatter_fusion = f32[20,128,128]{2,1,0:T(8,128)S(1)} fusion(f32[20,128,128]{2,1,0:T(8,128)S(1)} %broadcast.166.clone, s32[128]{0:T(128)S(1)} %fusion.50, f32[128,128,128]{2,1,0:T(8,128)} %copy.38), kind=kCustom, calls=%fused_computation.5 | custom fusion | flops 2097152 | bytes 25166336 | tf_op jit(solution)/shard_map/scatter-add | solution.py:87
  290.8 0.0 collective-permute-done.1
  290.8 3.0 fusion.61
  293.8 3.1 gather_fusion.3
  296.9 8.4 %convert_bitcast_fusion = f32[128,128,128]{1,2,0:T(8,128)} fusion(bf16[1,128,128,128]{3,2,1,0:T(8,128)(2,1)} %param.15, bf16[128,128,128]{2,1,0:T(8,128)(2,1)} %gather_fusion.3, pred[128]{0:T(512)(128)(4,1)S(1)} %copy-done.9), kind=kOutput, calls=%fused_computation.9 | convolution fusion | flops 543162368 | bytes 16777344 | tf_op jit(solution)/shard_map/snij,snic->snjc/dot_general | solution.py:47
  305.2 9.4 %copy.40 = f32[128,128,128]{0,2,1:T(8,128)} copy(f32[128,128,128]{1,2,0:T(8,128)} %convert_bitcast_fusion) | data formatting | bytes 16777216 | tf_op jit(solution)/shard_map/vmap()/convert_element_type | solution.py:58
  314.6 9.0 %copy.41 = f32[128,16384]{1,0:T(8,128)} copy(f32[128,16384]{0,1:T(8,128)} %bitcast.164) | data formatting | bytes 16777216 | tf_op jit(solution)/shard_map/vmap()/convert_element_type | solution.py:58
  323.7 15.1 %scatter_custom_fusion.3 = f32[64,16384]{1,0:T(8,128)} fusion(s32[128]{0:T(128)} %copy-done.14, f32[128,16384]{1,0:T(8,128)} %copy.41, f32[]{:T(128)} %constant.3.clone.1), kind=kCustom, calls=%fused_computation.37 | custom fusion | flops 2097152 | bytes 4194816 | tf_op jit(solution)/shard_map/vmap()/scatter-add | solution.py:57
  338.7 0.0 all-reduce.8.cloned.1.call-update
  338.8 0.0 all-gather.5.cloned.1.call-start
  338.8 110.8 %all-reduce.8.cloned.1.call-done = f32[64,1,16384]{2,0,1:T(8,128)} async-done(((f32[64,1,16384]{2,0,1:T(8,128)}), f32[64,1,16384]{2,0,1:T(8,128)}) %all-reduce.8.cloned.1.call-update) | async-done | bytes 4194320
  449.6 1.1 constant_dynamic-slice_fusion
  450.7 0.1 reshape_transpose.7
  450.8 0.8 subtract_convert_fusion
  451.6 0.0 all-gather.5.cloned.1.call-update
  451.6 2.5 collective-permute-start.2
  454.1 27.4 %collective-permute-done.2 = f32[1,2560,128]{2,1,0:T(8,128)S(1)} collective-permute-done((f32[1,2560,128]{2,1,0:T(8,128)S(1)}, f32[1,2560,128]{2,1,0:T(8,128)S(1)}, u32[]{:S(2)}, u32[]{:S(2)}) %collective-permute-start.2) | collective-permute-done | bytes 1310752 | tf_op jit(solution)/shard_map/ppermute | solution.py:13
  481.5 0.0 copy-done.2
  481.5 2.0 multiply_subtract_fusion
  483.5 1.2 collective-permute-start.3
  484.7 11.1 %all-gather.5.cloned.1.call-done = bf16[1,8192,128]{2,1,0:T(8,128)(2,1)} async-done(((bf16[1,256,128]{2,1,0:T(8,128)(2,1)}), bf16[1,8192,128]{2,1,0:T(8,128)(2,1)}) %all-gather.5.cloned.1.call-update) | async-done | bytes 2097168 | tf_op jit(solution)/shard_map/all_gather | solution.py:77
  495.8 4.8 gather_fusion.4
  500.5 9.9 %fusion.29 = f32[128,128,128]{1,2,0:T(8,128)} fusion(bf16[1,128,128,128]{3,2,1,0:T(8,128)(2,1)} %param.15, bf16[128,128,128]{2,1,0:T(8,128)(2,1)} %gather_fusion.4, pred[128]{0:T(512)(128)(4,1)S(1)} %copy-done.11), kind=kOutput, calls=%fused_computation.32 | convolution fusion | flops 538968064 | bytes 16777344 | tf_op jit(solution)/shard_map/snij,snjc->snic/dot_general | solution.py:81
  510.5 9.0 %copy.43 = f32[128,128,128]{2,1,0:T(8,128)} copy(f32[128,128,128]{1,2,0:T(8,128)} %fusion.29) | data formatting | bytes 16777216 | tf_op jit(solution)/shard_map/snij,snjc->snic/dot_general | solution.py:81
  519.4 0.1 broadcast.166
  519.6 0.0 copy-start.1
  519.6 17.0 %scatter_fusion.1 = f32[20,128,128]{2,1,0:T(8,128)S(1)} fusion(f32[20,128,128]{2,1,0:T(8,128)S(1)} %broadcast.166, s32[128]{0:T(128)S(1)} %copy-done.13, f32[128,128,128]{2,1,0:T(8,128)} %copy.43), kind=kCustom, calls=%fused_computation.6 | custom fusion | flops 2097152 | bytes 25166336 | tf_op jit(solution)/shard_map/scatter-add | solution.py:87
  536.6 0.0 collective-permute-done.3
  536.6 3.7 fusion.45
  (33 shorter events, 0.1 us)
Async XLA Ops:
  7.2 4.1 copy-start
  7.2 196.0 %all-reduce.6.cloned.1.call-start = ((), (), s32[]{:S(2)}) async-start(), calls=%async_computation.2 | async-start | bytes 8388608
  7.2 31.1 %collective-permute-start = (f32[1,2560,128]{2,1,0:T(8,128)}, f32[1,2560,128]{2,1,0:T(8,128)}, u32[]{:S(2)}, u32[]{:S(2)}) collective-permute-start(f32[1,2560,128]{2,1,0:T(8,128)} %param.25), channel_id=1, source_target_pairs={{0,96},{32,0},{64,32},{96,64},{1,97},{33,1},{65,33},{97,65},{2,98}... | collective-permute-start | bytes 3932168 | tf_op jit(solution)/shard_map/ppermute | solution.py:13
  15.3 30.1 %copy-start.8 = (pred[128]{0:T(512)(128)(4,1)}, pred[128]{0:T(512)(128)(4,1)S(1)}, u32[]{:S(2)}) copy-start(pred[128]{0:T(512)(128)(4,1)S(1)} %and_bitcast_fusion.1) | copy-start | bytes 388
  15.3 56.9 %copy-start.14 = (s32[128]{0:T(128)}, s32[128]{0:T(128)S(1)}, u32[]{:S(2)}) copy-start(s32[128]{0:T(128)S(1)} %fusion.51) | copy-start | bytes 1540
  42.3 162.9 %copy-start.3 = (f32[1,2560,128]{2,1,0:T(8,128)}, f32[1,2560,128]{2,1,0:T(8,128)S(1)}, u32[]{:S(2)}) copy-start(f32[1,2560,128]{2,1,0:T(8,128)S(1)} %get-tuple-element.11) | copy-start | bytes 3932164
  72.2 15.2 %copy-start.15 = (u32[128]{0:T(128)S(1)}, u32[128]{0:T(128)}, u32[]{:S(2)}) copy-start(u32[128]{0:T(128)} %constant.66) | copy-start | bytes 1540
  72.2 132.2 %copy-start.4 = (f32[1,256,128]{2,1,0:T(8,128)S(1)}, f32[1,256,128]{2,1,0:T(8,128)}, u32[]{:S(2)}) copy-start(f32[1,256,128]{2,1,0:T(8,128)} %param.23) | copy-start | bytes 393220
  72.2 132.2 %copy-start.6 = (f32[1,256]{1,0:T(1,128)S(1)}, f32[1,256]{1,0:T(1,128)}, u32[]{:S(2)}) copy-start(f32[1,256]{1,0:T(1,128)} %param.21) | copy-start | bytes 3076
  87.3 162.7 %all-gather.3.cloned.1.call-start = ((), (), s32[]{:S(2)}) async-start(), calls=%async_computation | async-start | bytes 2162688 | tf_op jit(solution)/shard_map/all_gather | solution.py:77
  205.2 244.4 %all-reduce.8.cloned.1.call-start = ((), (), s32[]{:S(2)}) async-start(), calls=%async_computation.3 | async-start | bytes 8388608
  205.2 85.5 %collective-permute-start.1 = (f32[1,2560,128]{2,1,0:T(8,128)S(1)}, f32[1,2560,128]{2,1,0:T(8,128)}, u32[]{:S(2)}, u32[]{:S(2)}) collective-permute-start(f32[1,2560,128]{2,1,0:T(8,128)S(1)} %get-tuple-element.11), channel_id=1, source_target_pairs={{0,32},{32,64},{64,96},{96,0},{1,33},{33,65},{65,97},{97,1},{2,34}... | collective-permute-start | bytes 3932168 | tf_op jit(solution)/shard_map/ppermute | solution.py:13
  207.0 47.6 %copy-start.5 = (s32[1024]{0:T(1024)}, s32[1024]{0:T(1024)S(1)}, u32[]{:S(2)}) copy-start(s32[1024]{0:T(1024)S(1)} %pad_clamp_fusion) | copy-start | bytes 12292
  207.1 47.6 %copy-start.10 = (pred[128]{0:T(512)(128)(4,1)}, pred[128]{0:T(512)(128)(4,1)S(1)}, u32[]{:S(2)}) copy-start(pred[128]{0:T(512)(128)(4,1)S(1)} %and_bitcast_fusion) | copy-start | bytes 388
  207.1 66.6 %copy-start.12 = (s32[128]{0:T(128)}, s32[128]{0:T(128)S(1)}, u32[]{:S(2)}) copy-start(s32[128]{0:T(128)S(1)} %fusion.50) | copy-start | bytes 1540
  293.8 3.1 copy-start.9
  323.7 127.2 %copy-start.7 = (f32[1,256]{1,0:T(1,128)S(1)}, f32[1,256]{1,0:T(1,128)}, u32[]{:S(2)}) copy-start(f32[1,256]{1,0:T(1,128)} %param.21) | copy-start | bytes 3076
  323.7 157.9 %copy-start.2 = (f32[1,2560,128]{2,1,0:T(8,128)S(1)}, f32[1,2560,128]{2,1,0:T(8,128)}, u32[]{:S(2)}) copy-start(f32[1,2560,128]{2,1,0:T(8,128)} %get-tuple-element.12) | copy-start | bytes 3932164
  338.8 157.0 %all-gather.5.cloned.1.call-start = ((), (), s32[]{:S(2)}) async-start(), calls=%async_computation.1 | async-start | bytes 2162688 | tf_op jit(solution)/shard_map/all_gather | solution.py:77
  451.6 29.9 %collective-permute-start.2 = (f32[1,2560,128]{2,1,0:T(8,128)S(1)}, f32[1,2560,128]{2,1,0:T(8,128)S(1)}, u32[]{:S(2)}, u32[]{:S(2)}) collective-permute-start(f32[1,2560,128]{2,1,0:T(8,128)S(1)} %get-tuple-element.10), channel_id=1, source_target_pairs={{0,96},{32,0},{64,32},{96,64},{1,97},{33,1},{65,33},{97,65},{2,98}... | collective-permute-start | bytes 3932168 | tf_op jit(solution)/shard_map/ppermute | solution.py:13
  483.5 53.1 %collective-permute-start.3 = (f32[1,2560,128]{2,1,0:T(8,128)}, f32[1,2560,128]{2,1,0:T(8,128)}, u32[]{:S(2)}, u32[]{:S(2)}) collective-permute-start(f32[1,2560,128]{2,1,0:T(8,128)} %get-tuple-element.7), channel_id=1, source_target_pairs={{0,32},{32,64},{64,96},{96,0},{1,33},{33,65},{65,97},{97,1},{2,34}... | collective-permute-start | bytes 3932168 | tf_op jit(solution)/shard_map/ppermute | solution.py:13
  495.8 4.8 copy-start.11
  510.4 9.1 %copy-start.13 = (s32[128]{0:T(128)S(1)}, s32[128]{0:T(128)}, u32[]{:S(2)}) copy-start(s32[128]{0:T(128)} %copy-done.12) | copy-start | bytes 1540
  519.6 20.8 %copy-start.1 = (s32[64]{0:T(128)S(1)}, s32[64]{0:T(128)}, u32[]{:S(2)}) copy-start(s32[64]{0:T(128)} %param.19) | copy-start | bytes 772
Sparse Core Ops, SparseCore 0:
  87.4 115.7 all-reduce.5
  206.0 43.9 all-gather.2
  338.9 110.6 all-reduce.7
  451.8 43.9 all-gather.4
where the time goes:
time: 553 us; the launch traced here: 547 us
  waiting for transfers between devices  330 us (60%)
  other arithmetic  81.8 us (15%)
  local copies, waits for them, and re-layouts  74.9 us (14%)
  matrix products  36.6 us (7%)
  between operations  14.9 us (3%)
  starting transfers between devices  8.97 us (2%)
    unnamed x6, waiting for transfers between devices  225 us
    all_gather x2, waiting for transfers between devices, per_device(): lax.all_gather(flows_bar, 'zone', axis=1, tiled=True)  54 us
    ppermute x4, waiting for transfers between devices, from_behind(): lax.ppermute(value, axis, [(i, (i + by) % size) for i in range(size)])  50.5 us
    convert_element_type x4, local copies, waits for them, and re-layouts, one_phase(): values.astype(jnp.float32)  36.8 us
    scatter-add x2, other arithmetic, per_device(): pushed = jnp.zeros((phase_count, band_tiles, tile_size, scenarios), jnp.f...  34.1 us
    scatter-add x3, other arithmetic, one_phase(): jax.ops.segment_sum(values.astype(jnp.float32), segment_ids, num_segments...  30.2 us
    dot_general x2, matrix products, per_device(): jnp.einsum('snij,snjc->snic', tiles, flow_picked, preferred_element_type=...  19.8 us
    dot_general x2, local copies, waits for them, and re-layouts, per_device(): jnp.einsum('snij,snjc->snic', tiles, flow_picked, preferred_element_type=...  18 us
  transfers between devices with their start and end apart: 8, of which 6 were waited for; matrix products, arithmetic and copies ran while one was open for 16% of the time, Pallas kernels for 0%

commit v1 on v0

--- a/solution.py
+++ b/solution.py
@@ -74,9 +74,9 @@
         )
         flows_bar = (2.0 * new_flows - flows).astype(jnp.bfloat16)
         stock_bar = 2.0 * new_stock - stock
-        gathered = lax.all_gather(flows_bar, "zone", axis=1, tiled=True).reshape(
-            phase_count, blocks_total, tile_size, scenarios
-        )
+        gathered = jnp.concatenate(
+            lax.all_to_all(jnp.stack([flows_bar] * lax.axis_size("zone")), "zone", 0, 0), axis=1
+        ).reshape(phase_count, blocks_total, tile_size, scenarios)
         flow_picked = jnp.take_along_axis(gathered, position[:, :, None, None], axis=1)
         products = jnp.einsum(
             "snij,snjc->snic", tiles, flow_picked, preferred_element_type=jnp.float32

time: 553 us -> 533 us (0.964)
  waiting for transfers between devices: 330 us -> 291 us
  starting transfers between devices: 8.97 us -> 20.6 us
    all_gather x2 -> x0, waiting for transfers between devices: 54 us -> none  [per_device(): lax.all_gather(flows_bar, 'zone', axis=1, tiled=True)]
    all_to_all x0 -> x2, waiting for transfers between devices: none -> 45.4 us  [per_device(): lax.all_to_all(jnp.stack([flows_bar] * lax.axis_size('zone')), 'zone', 0, 0)]
    ppermute x4, waiting for transfers between devices: 50.5 us -> 22.5 us  [from_behind(): lax.ppermute(value, axis, [(i, (i + by) % size) for i in range(size)])]
    all_to_all x0 -> x2, starting transfers between devices: none -> 11.9 us  [per_device(): lax.all_to_all(jnp.stack([flows_bar] * lax.axis_size('zone')), 'zone', 0, 0)]
    unnamed x6 -> x4, waiting for transfers between devices: 225 us -> 223 us
  transfers between devices with their start and end apart: 8 -> 8, of which waited for: 6 -> 5; matrix products, arithmetic and copies ran while one was open for 16% -> 18% of each run, Pallas kernels for 0% -> 0%
where the time goes in v1:
time: 533 us; the launch traced here: 526 us
  waiting for transfers between devices  291 us (55%)
  other arithmetic  86.3 us (16%)
  local copies, waits for them, and re-layouts  76 us (14%)
  matrix products  36.6 us (7%)
  starting transfers between devices  20.6 us (4%)
  between operations  15.2 us (3%)
    unnamed x4, waiting for transfers between devices  223 us
    all_to_all x2, waiting for transfers between devices, per_device(): lax.all_to_all(jnp.stack([flows_bar] * lax.axis_size('zone')), 'zone', 0, 0)  45.4 us
    convert_element_type x4, local copies, waits for them, and re-layouts, one_phase(): values.astype(jnp.float32)  36.7 us
    scatter-add x2, other arithmetic, per_device(): pushed = jnp.zeros((phase_count, band_tiles, tile_size, scenarios), jnp.f...  34.1 us
    scatter-add x3, other arithmetic, one_phase(): jax.ops.segment_sum(values.astype(jnp.float32), segment_ids, num_segments...  30.3 us
    ppermute x4, waiting for transfers between devices, from_behind(): lax.ppermute(value, axis, [(i, (i + by) % size) for i in range(size)])  22.5 us
    dot_general x2, matrix products, per_device(): jnp.einsum('snij,snjc->snic', tiles, flow_picked, preferred_element_type=...  19.8 us
    dot_general x2, local copies, waits for them, and re-layouts, per_device(): jnp.einsum('snij,snjc->snic', tiles, flow_picked, preferred_element_type=...  17.9 us
  transfers between devices with their start and end apart: 8, of which 5 were waited for; matrix products, arithmetic and copies ran while one was open for 18% of the time, Pallas kernels for 0%

profile of v1, /device:TPU:1, one launch (start us, length us, event | category | flops | bytes accessed | tf_op | source)
XLA Modules:
  0.0 525.8 jit_solution(687811972024966198)
XLA Ops:
  7.2 0.0 copy-start
  7.2 0.0 all-reduce.6.cloned.1.call-start
  7.2 3.4 collective-permute-start
  10.6 0.7 fusion.54
  11.3 1.2 gather_fusion
  12.5 0.7 reduce
  13.3 0.7 fusion.56
  13.9 0.6 pad_bitcast_fusion
  14.5 0.7 fusion.57
  15.2 0.7 and_bitcast_fusion.1
  15.9 22.5 %collective-permute-done = f32[1,2560,128]{2,1,0:T(8,128)S(1)} collective-permute-done((f32[1,2560,128]{2,1,0:T(8,128)}, f32[1,2560,128]{2,1,0:T(8,128)S(1)}, u32[]{:S(2)}, u32[]{:S(2)}) %collective-permute-start) | collective-permute-done | bytes 1310752 | tf_op jit(solution)/shard_map/ppermute | solution.py:13
  38.4 3.6 multiply_subtract_fusion.1
  42.0 3.0 gather_fusion.1
  45.0 8.4 %convert_bitcast_fusion.1 = f32[128,128,128]{1,2,0:T(8,128)} fusion(bf16[1,128,128,128]{3,2,1,0:T(8,128)(2,1)} %param.15, bf16[128,128,128]{2,1,0:T(8,128)(2,1)} %gather_fusion.1, pred[128]{0:T(512)(128)(4,1)S(1)} %and_bitcast_fusion.1), kind=kOutput, calls=%fused_computation.10 | convolution fusion | flops 543162368 | bytes 16777344 | tf_op jit(solution)/shard_map/snij,snic->snjc/dot_general | solution.py:47
  53.4 9.3 %copy.35 = f32[128,128,128]{0,2,1:T(8,128)} copy(f32[128,128,128]{1,2,0:T(8,128)} %convert_bitcast_fusion.1) | data formatting | bytes 16777216 | tf_op jit(solution)/shard_map/vmap()/convert_element_type | solution.py:58
  62.7 9.0 %copy.36 = f32[128,16384]{1,0:T(8,128)} copy(f32[128,16384]{0,1:T(8,128)} %bitcast.167) | data formatting | bytes 16777216 | tf_op jit(solution)/shard_map/vmap()/convert_element_type | solution.py:58
  71.7 0.0 copy-start.5
  71.7 15.3 %scatter_custom_fusion.2 = f32[64,16384]{1,0:T(8,128)} fusion(s32[128]{0:T(128)S(1)} %fusion.53, f32[128,16384]{1,0:T(8,128)} %copy.36, f32[]{:T(128)} %constant.3.clone.1), kind=kCustom, calls=%fused_computation.39 | custom fusion | flops 2097152 | bytes 4194816 | tf_op jit(solution)/shard_map/vmap()/scatter-add | solution.py:57
  87.0 0.0 all-reduce.6.cloned.1.call-update
  87.1 0.6 dynamic-slice
  88.4 114.5 %all-reduce.6.cloned.1.call-done = f32[64,1,16384]{2,0,1:T(8,128)} async-done(((f32[64,1,16384]{2,0,1:T(8,128)}), f32[64,1,16384]{2,0,1:T(8,128)}) %all-reduce.6.cloned.1.call-update) | async-done | bytes 4194320
  202.9 1.1 constant_dynamic-slice_fusion.1
  204.0 0.1 reshape_transpose.6
  204.1 0.1 fusion.50
  204.2 1.8 stack.4
  206.1 5.9 %all-to-all-start = ((bf16[32,1,256,128]{3,2,1,0:T(8,128)(2,1)}), bf16[32,1,256,128]{3,2,1,0:T(8,128)(2,1)S(1)}, u32[]{:S(2)}, u32[]{:S(2)}) async-start(bf16[32,1,256,128]{3,2,1,0:T(8,128)(2,1)} %stack.4), calls=%async_computation | async-start | bytes 4194304 | tf_op jit(solution)/shard_map/all_to_all | solution.py:78
  212.0 0.0 all-reduce.8.cloned.1.call-start
  212.1 1.4 collective-permute-start.1
  213.5 0.6 fusion.58
  214.1 0.6 pad_clamp_fusion
  214.7 1.2 and_bitcast_fusion
  215.9 1.3 fusion.52
  217.2 22.6 %all-to-all-done = bf16[32,1,256,128]{3,2,1,0:T(8,128)(2,1)S(1)} async-done(((bf16[32,1,256,128]{3,2,1,0:T(8,128)(2,1)}), bf16[32,1,256,128]{3,2,1,0:T(8,128)(2,1)S(1)}, u32[]{:S(2)}, u32[]{:S(2)}) %all-to-all-start) | async-done | bytes 2097184 | tf_op jit(solution)/shard_map/all_to_all | solution.py:78
  239.9 3.2 gather_fusion.2
  243.0 9.9 %fusion.20 = f32[128,128,128]{1,2,0:T(8,128)} fusion(bf16[1,128,128,128]{3,2,1,0:T(8,128)(2,1)} %param.15, bf16[128,128,128]{2,1,0:T(8,128)(2,1)} %gather_fusion.2, pred[128]{0:T(512)(128)(4,1)} %and_bitcast_fusion), kind=kOutput, calls=%fused_computation.31 | convolution fusion | flops 538968064 | bytes 16777344 | tf_op jit(solution)/shard_map/snij,snjc->snic/dot_general | solution.py:81
  252.9 9.0 %copy.38 = f32[128,128,128]{2,1,0:T(8,128)} copy(f32[128,128,128]{1,2,0:T(8,128)} %fusion.20) | data formatting | bytes 16777216 | tf_op jit(solution)/shard_map/snij,snjc->snic/dot_general | solution.py:81
  261.9 0.1 broadcast.172.clone
  262.1 17.0 %scatter_fusion = f32[20,128,128]{2,1,0:T(8,128)S(1)} fusion(f32[20,128,128]{2,1,0:T(8,128)S(1)} %broadcast.172.clone, s32[128]{0:T(128)S(1)} %copy-done.10, f32[128,128,128]{2,1,0:T(8,128)} %copy.38), kind=kCustom, calls=%fused_computation.5 | custom fusion | flops 2097152 | bytes 25166336 | tf_op jit(solution)/shard_map/scatter-add | solution.py:87
  279.1 0.0 collective-permute-done.1
  279.1 3.0 fusion.63
  282.1 3.1 gather_fusion.3
  285.2 8.4 %convert_bitcast_fusion = f32[128,128,128]{1,2,0:T(8,128)} fusion(bf16[1,128,128,128]{3,2,1,0:T(8,128)(2,1)} %param.15, bf16[128,128,128]{2,1,0:T(8,128)(2,1)} %gather_fusion.3, pred[128]{0:T(512)(128)(4,1)S(1)} %copy-done.8), kind=kOutput, calls=%fused_computation.9 | convolution fusion | flops 543162368 | bytes 16777344 | tf_op jit(solution)/shard_map/snij,snic->snjc/dot_general | solution.py:47
  293.6 9.3 %copy.40 = f32[128,128,128]{0,2,1:T(8,128)} copy(f32[128,128,128]{1,2,0:T(8,128)} %convert_bitcast_fusion) | data formatting | bytes 16777216 | tf_op jit(solution)/shard_map/vmap()/convert_element_type | solution.py:58
  302.9 9.0 %copy.41 = f32[128,16384]{1,0:T(8,128)} copy(f32[128,16384]{0,1:T(8,128)} %bitcast.168) | data formatting | bytes 16777216 | tf_op jit(solution)/shard_map/vmap()/convert_element_type | solution.py:58
  311.9 15.0 %scatter_custom_fusion.3 = f32[64,16384]{1,0:T(8,128)} fusion(s32[128]{0:T(128)} %copy-done.13, f32[128,16384]{1,0:T(8,128)} %copy.41, f32[]{:T(128)} %constant.3.clone.1), kind=kCustom, calls=%fused_computation.37 | custom fusion | flops 2097152 | bytes 4194816 | tf_op jit(solution)/shard_map/vmap()/scatter-add | solution.py:57
  326.9 0.0 all-reduce.8.cloned.1.call-update
  326.9 2.5 collective-permute-start.2
  329.3 108.6 %all-reduce.8.cloned.1.call-done = f32[64,1,16384]{2,0,1:T(8,128)} async-done(((f32[64,1,16384]{2,0,1:T(8,128)}), f32[64,1,16384]{2,0,1:T(8,128)}) %all-reduce.8.cloned.1.call-update) | async-done | bytes 4194320
  438.0 1.1 constant_dynamic-slice_fusion
  439.1 0.1 reshape_transpose.7
  439.2 0.8 fusion.51
  440.0 1.8 stack.5
  441.8 5.9 %all-to-all-start.1 = ((bf16[32,1,256,128]{3,2,1,0:T(8,128)(2,1)}), bf16[32,1,256,128]{3,2,1,0:T(8,128)(2,1)S(1)}, u32[]{:S(2)}, u32[]{:S(2)}) async-start(bf16[32,1,256,128]{3,2,1,0:T(8,128)(2,1)} %stack.5), calls=%async_computation.1 | async-start | bytes 4194304 | tf_op jit(solution)/shard_map/all_to_all | solution.py:78
  447.7 0.0 collective-permute-done.2
  447.7 3.6 multiply_subtract_fusion
  451.4 1.4 collective-permute-start.3
  452.8 22.8 %all-to-all-done.1 = bf16[32,1,256,128]{3,2,1,0:T(8,128)(2,1)S(1)} async-done(((bf16[32,1,256,128]{3,2,1,0:T(8,128)(2,1)}), bf16[32,1,256,128]{3,2,1,0:T(8,128)(2,1)S(1)}, u32[]{:S(2)}, u32[]{:S(2)}) %all-to-all-start.1) | async-done | bytes 2097184 | tf_op jit(solution)/shard_map/all_to_all | solution.py:78
  475.6 3.3 gather_fusion.4
  478.9 9.9 %fusion.29 = f32[128,128,128]{1,2,0:T(8,128)} fusion(bf16[1,128,128,128]{3,2,1,0:T(8,128)(2,1)} %param.15, bf16[128,128,128]{2,1,0:T(8,128)(2,1)} %gather_fusion.4, pred[128]{0:T(512)(128)(4,1)S(1)} %copy-done.9), kind=kOutput, calls=%fused_computation.32 | convolution fusion | flops 538968064 | bytes 16777344 | tf_op jit(solution)/shard_map/snij,snjc->snic/dot_general | solution.py:81
  488.8 9.0 %copy.43 = f32[128,128,128]{2,1,0:T(8,128)} copy(f32[128,128,128]{1,2,0:T(8,128)} %fusion.29) | data formatting | bytes 16777216 | tf_op jit(solution)/shard_map/snij,snjc->snic/dot_general | solution.py:81
  497.8 0.1 broadcast.172
  497.9 0.0 copy-start.1
  497.9 17.0 %scatter_fusion.1 = f32[20,128,128]{2,1,0:T(8,128)S(1)} fusion(f32[20,128,128]{2,1,0:T(8,128)S(1)} %broadcast.172, s32[128]{0:T(128)S(1)} %copy-done.11, f32[128,128,128]{2,1,0:T(8,128)} %copy.43), kind=kCustom, calls=%fused_computation.6 | custom fusion | flops 2097152 | bytes 25166336 | tf_op jit(solution)/shard_map/scatter-add | solution.py:87
  515.0 3.7 fusion.45
  (31 shorter events, 0.1 us)
Async XLA Ops:
  7.2 4.1 copy-start
  7.2 195.7 %all-reduce.6.cloned.1.call-start = ((), (), s32[]{:S(2)}) async-start(), calls=%async_computation.2 | async-start | bytes 8388608
  7.2 31.1 %collective-permute-start = (f32[1,2560,128]{2,1,0:T(8,128)}, f32[1,2560,128]{2,1,0:T(8,128)S(1)}, u32[]{:S(2)}, u32[]{:S(2)}) collective-permute-start(f32[1,2560,128]{2,1,0:T(8,128)} %param.25), channel_id=1, source_target_pairs={{0,96},{32,0},{64,32},{96,64},{1,97},{33,1},{65,33},{97,65},{2,98}... | collective-permute-start | bytes 3932168 | tf_op jit(solution)/shard_map/ppermute | solution.py:13
  12.5 3.3 copy-start.12
  15.8 29.2 %copy-start.7 = (pred[128]{0:T(512)(128)(4,1)}, pred[128]{0:T(512)(128)(4,1)S(1)}, u32[]{:S(2)}) copy-start(pred[128]{0:T(512)(128)(4,1)S(1)} %and_bitcast_fusion.1) | copy-start | bytes 388
  15.8 55.9 %copy-start.13 = (s32[128]{0:T(128)}, s32[128]{0:T(128)S(1)}, u32[]{:S(2)}) copy-start(s32[128]{0:T(128)S(1)} %fusion.53) | copy-start | bytes 1540
  42.0 170.1 %copy-start.2 = (f32[1,2560,128]{2,1,0:T(8,128)}, f32[1,2560,128]{2,1,0:T(8,128)S(1)}, u32[]{:S(2)}) copy-start(f32[1,2560,128]{2,1,0:T(8,128)S(1)} %get-tuple-element.11) | copy-start | bytes 3932164
  71.7 15.3 %copy-start.14 = (u32[128]{0:T(128)S(1)}, u32[128]{0:T(128)}, u32[]{:S(2)}) copy-start(u32[128]{0:T(128)} %constant.66) | copy-start | bytes 1540
  71.7 132.4 %copy-start.3 = (f32[1,256,128]{2,1,0:T(8,128)S(1)}, f32[1,256,128]{2,1,0:T(8,128)}, u32[]{:S(2)}) copy-start(f32[1,256,128]{2,1,0:T(8,128)} %param.23) | copy-start | bytes 393220
  71.7 132.4 %copy-start.5 = (f32[1,256]{1,0:T(1,128)S(1)}, f32[1,256]{1,0:T(1,128)}, u32[]{:S(2)}) copy-start(f32[1,256]{1,0:T(1,128)} %param.21) | copy-start | bytes 3076
  206.1 33.8 %all-to-all-start = ((bf16[32,1,256,128]{3,2,1,0:T(8,128)(2,1)}), bf16[32,1,256,128]{3,2,1,0:T(8,128)(2,1)S(1)}, u32[]{:S(2)}, u32[]{:S(2)}) async-start(bf16[32,1,256,128]{3,2,1,0:T(8,128)(2,1)} %stack.4), calls=%async_computation | async-start | bytes 4194304 | tf_op jit(solution)/shard_map/all_to_all | solution.py:78
  212.0 226.0 %all-reduce.8.cloned.1.call-start = ((), (), s32[]{:S(2)}) async-start(), calls=%async_computation.3 | async-start | bytes 8388608
  212.1 67.0 %collective-permute-start.1 = (f32[1,2560,128]{2,1,0:T(8,128)S(1)}, f32[1,2560,128]{2,1,0:T(8,128)}, u32[]{:S(2)}, u32[]{:S(2)}) collective-permute-start(f32[1,2560,128]{2,1,0:T(8,128)S(1)} %get-tuple-element.11), channel_id=1, source_target_pairs={{0,32},{32,64},{64,96},{96,0},{1,33},{33,65},{65,97},{97,1},{2,34}... | collective-permute-start | bytes 3932168 | tf_op jit(solution)/shard_map/ppermute | solution.py:13
  252.9 9.1 %copy-start.10 = (s32[128]{0:T(128)S(1)}, s32[128]{0:T(128)}, u32[]{:S(2)}) copy-start(s32[128]{0:T(128)} %fusion.52) | copy-start | bytes 1540
  282.1 3.1 copy-start.8
  311.9 127.3 %copy-start.4 = (f32[1,256,128]{2,1,0:T(8,128)S(1)}, f32[1,256,128]{2,1,0:T(8,128)}, u32[]{:S(2)}) copy-start(f32[1,256,128]{2,1,0:T(8,128)} %param.23) | copy-start | bytes 393220
  311.9 127.3 %copy-start.6 = (f32[1,256]{1,0:T(1,128)S(1)}, f32[1,256]{1,0:T(1,128)}, u32[]{:S(2)}) copy-start(f32[1,256]{1,0:T(1,128)} %param.21) | copy-start | bytes 3076
  326.9 120.8 %collective-permute-start.2 = (f32[1,2560,128]{2,1,0:T(8,128)S(1)}, f32[1,2560,128]{2,1,0:T(8,128)}, u32[]{:S(2)}, u32[]{:S(2)}) collective-permute-start(f32[1,2560,128]{2,1,0:T(8,128)S(1)} %get-tuple-element.10), channel_id=1, source_target_pairs={{0,96},{32,0},{64,32},{96,64},{1,97},{33,1},{65,33},{97,65},{2,98}... | collective-permute-start | bytes 3932168 | tf_op jit(solution)/shard_map/ppermute | solution.py:13
  441.8 33.8 %all-to-all-start.1 = ((bf16[32,1,256,128]{3,2,1,0:T(8,128)(2,1)}), bf16[32,1,256,128]{3,2,1,0:T(8,128)(2,1)S(1)}, u32[]{:S(2)}, u32[]{:S(2)}) async-start(bf16[32,1,256,128]{3,2,1,0:T(8,128)(2,1)} %stack.5), calls=%async_computation.1 | async-start | bytes 4194304 | tf_op jit(solution)/shard_map/all_to_all | solution.py:78
  451.4 63.6 %collective-permute-start.3 = (f32[1,2560,128]{2,1,0:T(8,128)}, f32[1,2560,128]{2,1,0:T(8,128)}, u32[]{:S(2)}, u32[]{:S(2)}) collective-permute-start(f32[1,2560,128]{2,1,0:T(8,128)} %get-tuple-element.7), channel_id=1, source_target_pairs={{0,32},{32,64},{64,96},{96,0},{1,33},{33,65},{65,97},{97,1},{2,34}... | collective-permute-start | bytes 3932168 | tf_op jit(solution)/shard_map/ppermute | solution.py:13
  475.6 3.3 copy-start.9
  488.8 9.1 %copy-start.11 = (s32[128]{0:T(128)S(1)}, s32[128]{0:T(128)}, u32[]{:S(2)}) copy-start(s32[128]{0:T(128)} %fusion.52) | copy-start | bytes 1540
  497.9 20.8 %copy-start.1 = (s32[64]{0:T(128)S(1)}, s32[64]{0:T(128)}, u32[]{:S(2)}) copy-start(s32[64]{0:T(128)} %param.19) | copy-start | bytes 772
Sparse Core Ops, SparseCore 0:
  87.2 115.6 all-reduce.5
  327.0 110.9 all-reduce.7
